TPU v7x, 512 devices: a whole 4x4x16 slice. The times are simulated.
512 devices in a mesh: neuron: 16 (over z), tm: 32 (over y, x, core).
Axes of the slice: x: 4, y: 4, z: 16, core: 2. Of those that a mesh axis runs over, the one named last changes fastest.
Arguments:
- spikes: int32 [65536, 8192], P('neuron', 'tm'), may hold values from 0 to 7
- read_weight: bfloat16 [65536, 256], P('neuron')
- in_proj: bfloat16 [256, 2048], P(None, 'neuron'), may hold values from -0.375 to 0.375
- decay_rate: float32 [2048], P('neuron'), may hold values from 1.2207031e-05 to 0.0333333333
- gate: float32 [8192], P('tm'), may hold values from 0.65 to 1
- out_fwd: bfloat16 [2048, 256], P('neuron'), may hold values from -0.125 to 0.125
- out_bwd: bfloat16 [2048, 256], P('neuron'), may hold values from -0.125 to 0.125
Outputs:
- latent: bfloat16 [8192, 256], P('tm')
- nll: float32 [65536], P('neuron')
All inputs are finite; a program needn't handle non-finite values.
Results may differ from a plain program's by a relative error of at most 0.011.
Values may be sent and summed in bfloat16 or wider, within the bound.
No kernel may reach another device: no remote copies, remote signals or barrier semaphores. Data moves between devices by JAX's collectives and lax.ppermute only.
A program may use at most 64 MiB of HBM per device.

v0:
```python
import jax
import jax.numpy as jnp
from jax import lax
from jax.sharding import PartitionSpec as P


def prefix(part, axis, combine, identity, reverse):
    count = lax.axis_size(axis)
    place = lax.axis_index(axis)
    ahead = count - 1 - place if reverse else place
    gathered = jax.tree.map(lambda a: lax.all_gather(a, axis), part)
    state = jax.tree.map(lambda a, e: jnp.zeros_like(a) + jnp.asarray(e, a.dtype), part, identity)

    def one(turn, state):
        source = count - 1 - turn if reverse else turn
        return combine(
            state, jax.tree.map(lambda a: lax.dynamic_index_in_dim(a, source, 0, False), gathered)
        )

    return lax.fori_loop(0, ahead, one, state)


def combine(earlier, later):
    return (earlier[0] * later[0], later[0] * earlier[1] + later[1])


def rms_round(rows):
    power = jnp.mean(rows * rows, axis=-1, keepdims=True) + 1e-05
    return (rows * lax.rsqrt(power)).astype(jnp.bfloat16)


def body(spikes, read_weight, in_proj, decay_rate, gate, out_fwd, out_bwd):
    counts = spikes.astype(jnp.bfloat16)
    partial_sum = lax.dot_general(
        counts, read_weight, (((0,), (0,)), ((), ())), preferred_element_type=jnp.float32
    )
    readin = lax.psum(partial_sum, "neuron")
    normed = rms_round(readin)
    scale_in = jnp.sqrt(-jnp.expm1(-2.0 * decay_rate))
    drive = jnp.dot(normed, in_proj, preferred_element_type=jnp.float32) * scale_in[None, :]
    step = jnp.exp(-decay_rate)[None, :] * gate[:, None]
    cum_fwd, state_fwd = lax.associative_scan(combine, (step, drive), axis=0)
    flipped = lax.associative_scan(combine, (jnp.flip(step, 0), jnp.flip(drive, 0)), axis=0)
    cum_bwd = jnp.flip(flipped[0], 0)
    state_bwd = jnp.flip(flipped[1], 0)
    block_decay = cum_fwd[-1]
    ones = jnp.ones_like(block_decay)
    zeros = jnp.zeros_like(block_decay)
    enter_fwd = prefix((block_decay, state_fwd[-1]), "tm", combine, (ones, zeros), False)[1]
    enter_bwd = prefix((block_decay, state_bwd[0]), "tm", combine, (ones, zeros), True)[1]
    forward = state_fwd + cum_fwd * enter_fwd[None, :]
    backward = state_bwd + cum_bwd * enter_bwd[None, :]
    mixed_part = jnp.dot(forward.astype(jnp.bfloat16), out_fwd, preferred_element_type=jnp.float32)
    mixed_part = mixed_part + jnp.dot(
        backward.astype(jnp.bfloat16), out_bwd, preferred_element_type=jnp.float32
    )
    mixed = lax.psum(mixed_part, "neuron")
    latent = (normed.astype(jnp.float32) + mixed).astype(jnp.bfloat16)
    log_rate = lax.dot_general(
        read_weight, latent, (((1,), (1,)), ((), ())), preferred_element_type=jnp.float32
    )
    terms = jnp.exp(log_rate) - spikes.astype(jnp.float32) * log_rate
    total = lax.psum(jnp.sum(terms, axis=1), "tm")
    nll = total / (spikes.shape[1] * lax.axis_size("tm"))
    return (latent, nll)


def solution(mesh):
    return jax.shard_map(
        body,
        mesh=mesh,
        in_specs=(
            P("neuron", "tm"),
            P("neuron", None),
            P(None, "neuron"),
            P("neuron"),
            P("tm"),
            P("neuron", None),
            P("neuron", None),
        ),
        out_specs=(P("tm", None), P("neuron")),
        check_vma=False,
    )
```

profile of v0, /device:TPU:32, one launch (start us, length us, event | category | flops | bytes accessed | tf_op | source)
XLA Modules:
  0.0 488.4 jit_solution(6418655048388268585)
XLA Ops:
  7.2 0.0 copy-start
  7.2 0.0 copy-start.7
  7.2 0.0 copy-start.6
  7.2 0.0 copy-start.5
  7.2 0.0 all-reduce.67.cloned.1.call-start
  7.3 1.5 copy-done
  8.8 3.6 fusion
  12.4 0.0 all-reduce.67.cloned.1.call-update
  12.4 0.0 all-reduce.69.cloned.1.call-start
  12.5 0.0 copy-done.7
  12.5 0.0 copy-done.6
  12.5 0.1 broadcast_multiply_fusion
  12.8 139.1 %all-reduce.67.cloned.1.call-done = f32[256,256]{1,0:T(8,128)} async-done(((f32[256,256]{1,0:T(8,128)}), f32[256,256]{1,0:T(8,128)}) %all-reduce.67.cloned.1.call-update) | async-done | bytes 262160 | tf_op jit(solution)/shard_map/psum | solution.py:37
  151.9 1.1 multiply_reduce_fusion
  152.9 0.0 copy-done.5
  152.9 1.2 convolution_multiply_fusion
  156.5 0.0 copy-start.3
  156.6 0.0 copy-start.4
  157.7 21.5 %all-gather.1 = f32[32,1,128]{2,1,0:T(1,128)S(1)} all-gather(f32[1,1,128]{2,1,0:T(1,128)S(1)} %add_bitcast_fusion.1), channel_id=1, replica_groups=mesh['neuron'=16,'tm'=32] {'tm'}, dimensions={0}, use_global_device_ids=true | all-gather | bytes 16896 | tf_op jit(solution)/shard_map/all_gather | solution.py:11
  179.3 20.2 %all-gather = f32[32,1,128]{2,1,0:T(1,128)S(1)} all-gather(f32[1,1,128]{2,1,0:T(1,128)S(1)} %add_bitcast_fusion.2), channel_id=1, replica_groups=mesh['neuron'=16,'tm'=32] {'tm'}, dimensions={0}, use_global_device_ids=true | all-gather | bytes 16896 | tf_op jit(solution)/shard_map/all_gather | solution.py:11
  199.5 0.1 rev.10
  199.6 0.1 rev.9
  199.7 20.7 %all-gather.2 = f32[32,1,128]{2,1,0:T(1,128)S(1)} all-gather(f32[1,1,128]{2,1,0:T(1,128)S(1)} %add_bitcast_fusion), channel_id=1, replica_groups=mesh['neuron'=16,'tm'=32] {'tm'}, dimensions={0}, use_global_device_ids=true | all-gather | bytes 16896 | tf_op jit(solution)/shard_map/all_gather | solution.py:11
  220.5 1.2 while.27
  221.7 0.0 copy-done.3
  221.7 0.2 fusion.2
  221.9 0.0 copy-done.4
  221.9 0.9 convolution_add_fusion
  222.7 0.0 all-reduce.69.cloned.1.call-update
  222.8 0.0 copy-start.1
  222.8 5.7 %copy.10 = s32[4096,256]{0,1:T(8,128)} copy(s32[4096,256]{1,0:T(8,128)} %param.11) | data formatting | bytes 8388608 | tf_op args[0]
  228.4 124.3 %all-reduce.69.cloned.1.call-done = f32[256,256]{1,0:T(8,128)} async-done(((f32[256,256]{1,0:T(8,128)}), f32[256,256]{1,0:T(8,128)}) %all-reduce.69.cloned.1.call-update) | async-done | bytes 262160 | tf_op jit(solution)/shard_map/psum | solution.py:57
  352.7 0.0 copy-done.1
  352.7 1.0 add_convert_fusion
  353.8 0.0 copy-start.2
  353.8 3.4 subtract_reduce_fusion
  357.2 123.8 %psum.23 = f32[4096]{0:T(1024)S(1)} all-reduce(f32[4096]{0:T(1024)S(1)} %subtract_reduce_fusion), channel_id=1, replica_groups=mesh['neuron'=16,'tm'=32] {'tm'}, use_global_device_ids=true, to_apply=%region_8.9 | all-reduce | flops 4096 | bytes 32768 | tf_op jit(solution)/shard_map/psum | solution.py:63
  480.9 0.6 broadcast_multiply_fusion.1
  481.6 0.0 copy-done.2
  (285 shorter events, 3.2 us)
Async XLA Ops:
  7.2 1.6 copy-start
  7.2 5.3 %copy-start.7 = (f32[128]{0:T(128)S(1)}, f32[128]{0:T(128)}, u32[]{:S(2)}) copy-start(f32[128]{0:T(128)} %param.14) | copy-start | bytes 1540
  7.2 5.3 %copy-start.6 = (f32[256]{0:T(256)S(1)}, f32[256]{0:T(256)}, u32[]{:S(2)}) copy-start(f32[256]{0:T(256)} %param.15) | copy-start | bytes 3076
  7.2 145.7 %copy-start.5 = (bf16[256,128]{1,0:T(8,128)(2,1)S(1)}, bf16[256,128]{1,0:T(8,128)(2,1)}, u32[]{:S(2)}) copy-start(bf16[256,128]{1,0:T(8,128)(2,1)} %param.13) | copy-start | bytes 196612
  7.2 144.6 %all-reduce.67.cloned.1.call-start = ((), (), s32[]{:S(2)}) async-start(), calls=%async_computation | async-start | bytes 524288 | tf_op jit(solution)/shard_map/psum | solution.py:37
  12.4 340.3 %all-reduce.69.cloned.1.call-start = ((), (), s32[]{:S(2)}) async-start(), calls=%async_computation.1 | async-start | bytes 524288 | tf_op jit(solution)/shard_map/psum | solution.py:57
  156.5 65.2 %copy-start.3 = (bf16[128,256]{1,0:T(8,128)(2,1)S(1)}, bf16[128,256]{1,0:T(8,128)(2,1)}, u32[]{:S(2)}) copy-start(bf16[128,256]{1,0:T(8,128)(2,1)} %param.16) | copy-start | bytes 196612
  156.6 65.2 %copy-start.4 = (bf16[128,256]{1,0:T(8,128)(2,1)S(1)}, bf16[128,256]{1,0:T(8,128)(2,1)}, u32[]{:S(2)}) copy-start(bf16[128,256]{1,0:T(8,128)(2,1)} %param.17) | copy-start | bytes 196612
  222.8 130.0 %copy-start.1 = (f32[256,256]{1,0:T(8,128)S(1)}, f32[256,256]{1,0:T(8,128)}, u32[]{:S(2)}) copy-start(f32[256,256]{1,0:T(8,128)} %all-reduce.67.cloned.1.call-done) | copy-start | bytes 786436
  353.8 127.8 %copy-start.2 = (bf16[256,256]{1,0:T(8,128)(2,1)}, bf16[256,256]{1,0:T(8,128)(2,1)S(1)}, u32[]{:S(2)}) copy-start(bf16[256,256]{1,0:T(8,128)(2,1)S(1)} %add_convert_fusion) | copy-start | bytes 393220
Sparse Core Ops, SparseCore 0:
  12.5 139.2 all-reduce.66
  222.9 129.8 all-reduce.68
where the time goes:
time: 489 us; the launch traced here: 488 us
  waiting for transfers between devices  263 us (54%)
  blocking collectives  186 us (38%)
  between operations  15.5 us (3%)
  local copies, waits for them, and re-layouts  9.21 us (2%)
  matrix products  9.19 us (2%)
    psum x1, waiting for transfers between devices, body(): readin = lax.psum(partial_sum, 'neuron')  139 us
    psum x1, waiting for transfers between devices, body(): mixed = lax.psum(mixed_part, 'neuron')  124 us
    psum x1, blocking collectives, body(): total = lax.psum(jnp.sum(terms, axis=1), 'tm')  124 us
    all_gather x3, blocking collectives, prefix(): gathered = jax.tree.map(lambda a: lax.all_gather(a, axis), part)  62.4 us
  transfers between devices with their start and end apart: 2, of which 2 were waited for; matrix products, arithmetic and copies ran while one was open for 1% of the time, Pallas kernels for 0%

commit v1 on v0

--- a/solution.py
+++ b/solution.py
@@ -34,7 +34,7 @@
     partial_sum = lax.dot_general(
         counts, read_weight, (((0,), (0,)), ((), ())), preferred_element_type=jnp.float32
     )
-    readin = lax.psum(partial_sum, "neuron")
+    readin = jnp.sum(lax.all_gather(partial_sum, "neuron"), axis=0)
     normed = rms_round(readin)
     scale_in = jnp.sqrt(-jnp.expm1(-2.0 * decay_rate))
     drive = jnp.dot(normed, in_proj, preferred_element_type=jnp.float32) * scale_in[None, :]

time: 489 us -> 462 us (0.945)
  waiting for transfers between devices: 263 us -> 207 us
  local copies, waits for them, and re-layouts: 9.21 us -> 26.8 us
  other arithmetic: 4.19 us -> 17.4 us
    psum x1 -> x0, waiting for transfers between devices: 139 us -> none  [body(): readin = lax.psum(partial_sum, 'neuron')]
    all_gather x0 -> x1, waiting for transfers between devices: none -> 82 us  [body(): readin = jnp.sum(lax.all_gather(partial_sum, 'neuron'), axis=0)]
    slice x54, local copies, waits for them, and re-layouts: 0.69 us -> 9.59 us  [body(): lax.associative_scan(combine, (jnp.flip(step, 0), jnp.flip(drive, 0)), ax...]
    slice x50, local copies, waits for them, and re-layouts: 0.63 us -> 8.93 us  [body(): cum_fwd, state_fwd = lax.associative_scan(combine, (step, drive), axis=0)]
    concatenate x14, other arithmetic: 0.13 us -> 7.88 us  [body(): lax.associative_scan(combine, (jnp.flip(step, 0), jnp.flip(drive, 0)), ax...]
where the time goes in v1:
time: 462 us; the launch traced here: 461 us
  waiting for transfers between devices  207 us (45%)
  blocking collectives  185 us (40%)
  local copies, waits for them, and re-layouts  26.8 us (6%)
  other arithmetic  17.4 us (4%)
  between operations  15.3 us (3%)
  matrix products  8.28 us (2%)
    psum x1, waiting for transfers between devices, body(): mixed = lax.psum(mixed_part, 'neuron')  125 us
    psum x1, blocking collectives, body(): total = lax.psum(jnp.sum(terms, axis=1), 'tm')  124 us
    all_gather x1, waiting for transfers between devices, body(): readin = jnp.sum(lax.all_gather(partial_sum, 'neuron'), axis=0)  82 us
    all_gather x3, blocking collectives, prefix(): gathered = jax.tree.map(lambda a: lax.all_gather(a, axis), part)  61.7 us
    slice x54, local copies, waits for them, and re-layouts, body(): lax.associative_scan(combine, (jnp.flip(step, 0), jnp.flip(drive, 0)), ax...  9.59 us
  transfers between devices with their start and end apart: 2, of which 2 were waited for; matrix products, arithmetic and copies ran while one was open for 1% of the time, Pallas kernels for 0%

profile of v1, /device:TPU:32, one launch (start us, length us, event | category | flops | bytes accessed | tf_op | source)
XLA Modules:
  0.0 461.0 jit_solution(7016346450091563856)
XLA Ops:
  7.2 1.5 copy-done
  8.8 3.7 fusion
  12.8 0.6 fusion.13
  13.4 82.0 %all-gather.6.cloned.1.call-done = f32[4096,256]{1,0:T(8,128)} async-done(((f32[256,256]{1,0:T(8,128)}), f32[4096,256]{1,0:T(8,128)}) %all-gather.6.cloned.1.call-update) | async-done | bytes 4194320 | tf_op jit(solution)/shard_map/all_gather | solution.py:37
  95.3 2.5 reduce_sum.27
  99.0 0.6 slice.598
  99.5 0.6 slice.599
  100.1 0.6 slice.597
  100.7 0.6 slice.601
  101.9 0.6 slice.624
  103.0 0.6 slice.682
  103.6 0.6 slice.668
  108.0 0.6 slice.521
  108.6 0.6 slice.522
  109.7 0.6 slice.524
  110.3 0.6 slice.513
  110.9 0.6 slice.530
  114.9 0.6 slice.650
  115.4 0.6 slice.637
  116.7 0.7 fusion.23
  117.6 0.6 pad_maximum_fusion.22
  118.2 0.7 pad_maximum_fusion.23
  119.0 0.6 pad_maximum_fusion.18
  119.6 0.7 pad_maximum_fusion.19
  120.3 0.7 pad_maximum_fusion.14
  121.0 0.7 pad_maximum_fusion.15
  121.8 0.6 pad_maximum_fusion.10
  122.4 0.6 pad_maximum_fusion.11
  123.1 0.7 pad_maximum_fusion.6
  123.9 0.6 pad_maximum_fusion.7
  124.6 0.6 pad_maximum_fusion.2
  125.3 21.5 %all-gather.3 = f32[32,1,128]{2,1,0:T(1,128)S(1)} all-gather(f32[1,1,128]{2,1,0:T(1,128)S(1)} %add_bitcast_fusion), channel_id=1, replica_groups=mesh['neuron'=16,'tm'=32] {'tm'}, dimensions={0}, use_global_device_ids=true | all-gather | bytes 16896 | tf_op jit(solution)/shard_map/all_gather | solution.py:11
  146.7 0.7 multiply_add_fusion.17
  147.6 0.7 pad_maximum_fusion.21
  148.3 0.7 pad_maximum_fusion.20
  149.7 0.6 pad_maximum_fusion.1
  150.3 20.2 %all-gather.1 = f32[32,1,128]{2,1,0:T(1,128)S(1)} all-gather(f32[1,1,128]{2,1,0:T(1,128)S(1)} %add_bitcast_fusion.2), channel_id=1, replica_groups=mesh['neuron'=16,'tm'=32] {'tm'}, dimensions={0}, use_global_device_ids=true | all-gather | bytes 16896 | tf_op jit(solution)/shard_map/all_gather | solution.py:11
  170.5 1.4 while.27
  171.9 0.7 pad_maximum_fusion.3
  172.8 0.6 pad_maximum_fusion
  173.5 20.0 %all-gather.2 = f32[32,1,128]{2,1,0:T(1,128)S(1)} all-gather(f32[1,1,128]{2,1,0:T(1,128)S(1)} %add_bitcast_fusion.1), channel_id=1, replica_groups=mesh['neuron'=16,'tm'=32] {'tm'}, dimensions={0}, use_global_device_ids=true | all-gather | bytes 16896 | tf_op jit(solution)/shard_map/all_gather | solution.py:11
  193.7 0.9 convolution_add_fusion
  194.6 5.7 %copy.10 = s32[4096,256]{0,1:T(8,128)} copy(s32[4096,256]{1,0:T(8,128)} %param.11) | data formatting | bytes 8388608 | tf_op args[0]
  200.3 125.1 %all-reduce.66.cloned.1.call-done = f32[256,256]{1,0:T(8,128)} async-done(((f32[256,256]{1,0:T(8,128)}), f32[256,256]{1,0:T(8,128)}) %all-reduce.66.cloned.1.call-update) | async-done | bytes 262160 | tf_op jit(solution)/shard_map/psum | solution.py:57
  325.4 1.0 add_convert_fusion
  326.5 3.4 subtract_reduce_fusion
  329.8 123.8 %psum.15 = f32[4096]{0:T(1024)S(1)} all-reduce(f32[4096]{0:T(1024)S(1)} %subtract_reduce_fusion), channel_id=1, replica_groups=mesh['neuron'=16,'tm'=32] {'tm'}, use_global_device_ids=true, to_apply=%region_8.9 | all-reduce | flops 4096 | bytes 32768 | tf_op jit(solution)/shard_map/psum | solution.py:63
  453.6 0.6 broadcast_multiply_fusion.1
  (297 shorter events, 12.6 us)
Async XLA Ops:
  7.2 1.6 copy-start
  7.2 5.3 %copy-start.17 = (f32[128]{0:T(128)S(1)}, f32[128]{0:T(128)}, u32[]{:S(2)}) copy-start(f32[128]{0:T(128)} %param.14) | copy-start | bytes 1540
  7.2 5.3 %copy-start.9 = (f32[256]{0:T(256)S(1)}, f32[256]{0:T(256)}, u32[]{:S(2)}) copy-start(f32[256]{0:T(256)} %param.15) | copy-start | bytes 3076
  7.2 88.1 %all-gather.6.cloned.1.call-start = ((), (), s32[]{:S(2)}) async-start(), calls=%async_computation.1 | async-start | bytes 4456448 | tf_op jit(solution)/shard_map/all_gather | solution.py:37
  12.4 85.6 %copy-start.4 = (bf16[256,128]{1,0:T(8,128)(2,1)S(1)}, bf16[256,128]{1,0:T(8,128)(2,1)}, u32[]{:S(2)}) copy-start(bf16[256,128]{1,0:T(8,128)(2,1)} %param.13) | copy-start | bytes 196612
  12.4 312.9 %all-reduce.66.cloned.1.call-start = ((), (), s32[]{:S(2)}) async-start(), calls=%async_computation | async-start | bytes 524288 | tf_op jit(solution)/shard_map/psum | solution.py:57
  98.0 0.6 copy-start.5
  116.6 31.0 %copy-start.7 = (f32[3,128]{1,0:T(4,128)S(1)}, f32[3,128]{1,0:T(4,128)}, u32[]{:S(2)}) copy-start(f32[3,128]{1,0:T(4,128)} %slice.513) | copy-start | bytes 4612
  116.6 31.0 %copy-start.8 = (f32[3,128]{1,0:T(4,128)S(1)}, f32[3,128]{1,0:T(4,128)}, u32[]{:S(2)}) copy-start(f32[3,128]{1,0:T(4,128)} %slice.530) | copy-start | bytes 4612
  116.6 32.5 %copy-start.16 = (f32[1,128]{1,0:T(1,128)S(1)}, f32[1,128]{1,0:T(1,128)}, u32[]{:S(2)}) copy-start(f32[1,128]{1,0:T(1,128)} %slice.652) | copy-start | bytes 1540
  116.6 32.5 %copy-start.15 = (f32[1,128]{1,0:T(1,128)S(1)}, f32[1,128]{1,0:T(1,128)}, u32[]{:S(2)}) copy-start(f32[1,128]{1,0:T(1,128)} %slice.639) | copy-start | bytes 1540
  116.6 32.6 %copy-start.14 = (f32[1,128]{1,0:T(1,128)S(1)}, f32[1,128]{1,0:T(1,128)}, u32[]{:S(2)}) copy-start(f32[1,128]{1,0:T(1,128)} %slice.651) | copy-start | bytes 1540
  116.6 32.6 %copy-start.13 = (f32[1,128]{1,0:T(1,128)S(1)}, f32[1,128]{1,0:T(1,128)}, u32[]{:S(2)}) copy-start(f32[1,128]{1,0:T(1,128)} %slice.638) | copy-start | bytes 1540
  116.6 32.7 %copy-start.12 = (f32[1,128]{1,0:T(1,128)S(1)}, f32[1,128]{1,0:T(1,128)}, u32[]{:S(2)}) copy-start(f32[1,128]{1,0:T(1,128)} %slice.650) | copy-start | bytes 1540
  116.6 32.8 %copy-start.11 = (f32[1,128]{1,0:T(1,128)S(1)}, f32[1,128]{1,0:T(1,128)}, u32[]{:S(2)}) copy-start(f32[1,128]{1,0:T(1,128)} %slice.637) | copy-start | bytes 1540
  116.6 32.8 %copy-start.10 = (f32[1,128]{1,0:T(1,128)S(1)}, f32[1,128]{1,0:T(1,128)}, u32[]{:S(2)}) copy-start(f32[1,128]{1,0:T(1,128)} %slice.649) | copy-start | bytes 1540
  123.1 70.4 %copy-start.2 = (bf16[128,256]{1,0:T(8,128)(2,1)S(1)}, bf16[128,256]{1,0:T(8,128)(2,1)}, u32[]{:S(2)}) copy-start(bf16[128,256]{1,0:T(8,128)(2,1)} %param.16) | copy-start | bytes 196612
  124.5 69.2 %copy-start.3 = (bf16[128,256]{1,0:T(8,128)(2,1)S(1)}, bf16[128,256]{1,0:T(8,128)(2,1)}, u32[]{:S(2)}) copy-start(bf16[128,256]{1,0:T(8,128)(2,1)} %param.17) | copy-start | bytes 196612
  194.6 130.8 %copy-start.6 = (f32[256]{0:T(256)S(1)}, f32[256]{0:T(256)}, u32[]{:S(2)}) copy-start(f32[256]{0:T(256)} %copy-done.5) | copy-start | bytes 3076
  326.4 127.8 %copy-start.1 = (bf16[256,256]{1,0:T(8,128)(2,1)}, bf16[256,256]{1,0:T(8,128)(2,1)S(1)}, u32[]{:S(2)}) copy-start(bf16[256,256]{1,0:T(8,128)(2,1)S(1)} %add_convert_fusion) | copy-start | bytes 393220
Sparse Core Ops, SparseCore 0:
  12.6 82.7 all-gather.5
  194.7 130.6 all-reduce.65
